TPU v7x, 512 devices: a whole 4x8x8 slice. The times are simulated.
512 devices in a mesh: kv: 8 (over z), wide: 64 (over x, y, core).
Axes of the slice: x: 4, y: 8, z: 8, core: 2. Of those that a mesh axis runs over, the one named last changes fastest.
Arguments:
- hidden_input: bfloat16 [192, 16384], P(None, 'kv'), may hold values from -6 to 6
- input_norm_gain: float32 [16384], P('kv'), may hold values from 0.25 to 1.75
- joint_projection_weight: bfloat16 [16384, 18432], P('kv', 'wide'), may hold values from -0.046875 to 0.046875
- output_weight: bfloat16 [16384, 16384], P('kv', 'wide'), may hold values from -0.046875 to 0.046875
- key_cache: bfloat16 [192, 8, 512, 128], P('wide', 'kv'), may hold values from -210 to 210
- value_cache: bfloat16 [192, 8, 512, 128], P('wide', 'kv'), may hold values from -6 to 6
- joint_down_weight: bfloat16 [64, 16384, 24], P('wide', 'kv'), may hold values from -0.046875 to 0.046875
- query_up_weight: bfloat16 [64, 8, 16384], P('wide', None, 'kv'), may hold values from -2 to 2
- key_value_up_weight: bfloat16 [64, 2, 8, 1024], P('wide', None, None, 'kv'), may hold values from -2 to 2
- output_down_weight: bfloat16 [64, 16384, 8], P('wide', 'kv'), may hold values from -0.046875 to 0.046875
- output_up_weight: bfloat16 [64, 8, 16384], P('wide'), may hold values from -2 to 2
- row_adapter_index: int32 [192], replicated, may hold values from 0 to 63
- adapter_owner_slot: int32 [64], replicated, may hold values from 0 to 63, each once
- lengths: int32 [192], P('wide'), may hold values from 64 to 512, as said below
Outputs:
- out: bfloat16 [192, 16384], P('kv', 'wide')
Inputs may be any that keep to these rules, and one draw needn't show every extreme that they name: Row lengths; at least one row has exactly 512. `adapter_owner_slot`: each adapter's owner slot, a permutation.
All inputs are finite; a program needn't handle non-finite values.
Results may differ from a plain program's by a relative error of at most 0.019.
The roundings to bfloat16 on the way count: a program that leaves them out, or rounds other values in their place, can miss the bound.
Values may be sent and summed in bfloat16 or wider, within the bound.
A program may use at most 128 MiB of HBM per device.

v0:
```python
import jax
import jax.numpy as jnp
from jax import lax
from jax.sharding import PartitionSpec as P

MODEL_WIDTH = 16384


rope_base = 500000.0
adapter_scale = 2.0


def rotate(values, positions):
    half = values.shape[-1] // 2
    freq = rope_base ** (-jnp.arange(half, dtype=jnp.float32) * 2.0 / values.shape[-1])
    angle = positions.astype(jnp.float32)[:, None] * freq[None, :]
    array_shape = (angle.shape[0],) + (1,) * (values.ndim - 2) + (half,)
    cosine = jnp.cos(angle).reshape(array_shape)
    sine = jnp.sin(angle).reshape(array_shape)
    first = values[..., :half]
    second = values[..., half:]
    return jnp.concatenate(
        [first * cosine - second * sine, second * cosine + first * sine], axis=-1
    )


def arrange(query_change, key_change, value_change, local_key_value):
    count = query_change.shape[0]
    joined = jnp.concatenate(
        [
            query_change.reshape(count, local_key_value, -1),
            key_change.reshape(count, local_key_value, -1),
            value_change.reshape(count, local_key_value, -1),
        ],
        axis=2,
    )
    return joined.reshape(count, -1)


def on_device(
    hidden_input,
    input_norm_gain,
    joint_projection_weight,
    output_weight,
    key_cache,
    value_cache,
    joint_down_weight,
    query_up_weight,
    key_value_up_weight,
    output_down_weight,
    output_up_weight,
    row_adapter_index,
    adapter_owner_slot,
    lengths,
):
    local_rows = lengths.shape[0]
    local_key_value = key_cache.shape[1]
    head_dim = key_cache.shape[3]
    rank_width = query_up_weight.shape[1]
    wide_pos = lax.axis_index("wide")
    kv_pos = lax.axis_index("kv")
    row_start = wide_pos * local_rows
    table = (
        row_adapter_index[:, None]
        == jnp.arange(adapter_owner_slot.shape[0], dtype=jnp.int32)[None, :]
    )
    row_slot = jnp.sum(jnp.where(table, adapter_owner_slot[None, :], 0), axis=1)
    mine = (row_slot == wide_pos).astype(jnp.float32)
    widened = hidden_input.astype(jnp.float32)
    scaled_hidden = (widened * input_norm_gain[None, :]).astype(jnp.bfloat16)
    partial_sq = jnp.sum(widened * widened, axis=1)
    partial_reduced = jnp.dot(
        scaled_hidden, joint_down_weight[0], preferred_element_type=jnp.float32
    )
    total_sq, reduced_hidden = lax.psum((partial_sq, partial_reduced), "kv")
    scale = lax.rsqrt(total_sq / MODEL_WIDTH + 1e-05)
    shrink_bf = (reduced_hidden * scale[:, None] * mine[:, None]).astype(jnp.bfloat16)
    base_part = jnp.dot(scaled_hidden, joint_projection_weight, preferred_element_type=jnp.float32)
    regrouped = lax.all_to_all(base_part, "wide", split_axis=0, concat_axis=1, tiled=True)
    grouped_heads = lax.psum_scatter(regrouped, "kv", scatter_dimension=1, tiled=True)
    row_scale = lax.dynamic_slice_in_dim(scale, row_start, local_rows)
    grouped_heads = grouped_heads * row_scale[:, None]
    shrinks = lax.all_gather(shrink_bf[None], "wide", axis=0, tiled=True)
    query_sheet = lax.all_gather(query_up_weight, "wide", axis=0, tiled=True)
    key_value_sheet = lax.all_gather(key_value_up_weight, "wide", axis=0, tiled=True)
    own_rows = lax.dynamic_slice_in_dim(shrinks, row_start, local_rows, 1)
    query_change = jnp.einsum(
        "nbr,nrc->bc", own_rows[:, :, :rank_width], query_sheet, preferred_element_type=jnp.float32
    )
    key_change = jnp.einsum(
        "nbr,nrc->bc",
        own_rows[:, :, rank_width : 2 * rank_width],
        key_value_sheet[:, 0],
        preferred_element_type=jnp.float32,
    )
    value_change = jnp.einsum(
        "nbr,nrc->bc",
        own_rows[:, :, 2 * rank_width :],
        key_value_sheet[:, 1],
        preferred_element_type=jnp.float32,
    )
    adapter_change = arrange(query_change, key_change, value_change, local_key_value)
    merged_output = (grouped_heads + adapter_scale * adapter_change).reshape(
        local_rows, local_key_value, -1
    )
    width = merged_output.shape[2] - 2 * head_dim
    heads_per = width // head_dim
    query_vector = rotate(
        merged_output[:, :, :width].reshape(local_rows, local_key_value, heads_per, head_dim),
        lengths,
    ).astype(jnp.bfloat16)
    fresh_key = rotate(merged_output[:, :, width : width + head_dim], lengths).astype(jnp.bfloat16)
    value_new = merged_output[:, :, width + head_dim :].astype(jnp.bfloat16)
    inverse_root = jnp.sqrt(jnp.float32(head_dim))
    scores = (
        jnp.einsum("rkgd,rkld->rkgl", query_vector, key_cache, preferred_element_type=jnp.float32)
        / inverse_root
    )
    valid = jnp.arange(key_cache.shape[2], dtype=jnp.int32)[None, :] < lengths[:, None]
    scores = jnp.where(valid[:, None, None, :], scores, -jnp.inf)
    fresh_score = (
        jnp.einsum("rkgd,rkd->rkg", query_vector, fresh_key, preferred_element_type=jnp.float32)
        / inverse_root
    )
    top = jnp.maximum(jnp.max(scores, axis=-1), fresh_score)
    expd = jnp.exp(scores - top[..., None])
    exp_new = jnp.exp(fresh_score - top)
    total = jnp.sum(expd, axis=-1) + exp_new
    probs = (expd / total[..., None]).astype(jnp.bfloat16)
    prob_new = (exp_new / total).astype(jnp.bfloat16)
    attention_output = jnp.einsum(
        "rkgl,rkld->rkgd", probs, value_cache, preferred_element_type=jnp.float32
    )
    attention_output = (
        attention_output
        + prob_new.astype(jnp.float32)[..., None] * value_new.astype(jnp.float32)[:, :, None, :]
    )
    attention_output = attention_output.astype(jnp.bfloat16).reshape(local_rows, -1)
    out_cols = output_weight.shape[1]
    slice_portion = lax.all_gather(attention_output, "wide", axis=0, tiled=True)
    mixed = jnp.concatenate(
        [
            jnp.dot(slice_portion, output_weight, preferred_element_type=jnp.float32),
            jnp.dot(slice_portion, output_down_weight[0], preferred_element_type=jnp.float32),
        ],
        axis=1,
    )
    output_baseline = lax.psum_scatter(
        mixed[:, :out_cols].astype(jnp.bfloat16), "kv", scatter_dimension=0, tiled=True
    ).astype(jnp.float32)
    output_reduced = lax.psum(mixed[:, out_cols:], "kv")
    block = output_baseline.shape[0]
    own_shrink = lax.dynamic_slice_in_dim(
        output_reduced * mine[:, None], kv_pos * block, block, 0
    ).astype(jnp.bfloat16)
    weight_sheet = output_up_weight[0]
    output_change = lax.psum_scatter(
        jnp.dot(weight_sheet.T, own_shrink.T, preferred_element_type=jnp.float32),
        "wide",
        scatter_dimension=0,
        tiled=True,
    )
    return (output_baseline + adapter_scale * output_change.T).astype(jnp.bfloat16)


def solution(mesh):
    in_specs = (
        P(None, "kv"),
        P("kv"),
        P("kv", "wide"),
        P("kv", "wide"),
        P("wide", "kv", None, None),
        P("wide", "kv", None, None),
        P("wide", "kv", None),
        P("wide", None, "kv"),
        P("wide", None, None, "kv"),
        P("wide", "kv", None),
        P("wide", None, None),
        P(),
        P(),
        P("wide"),
    )
    out_specs = P("kv", "wide")
    return jax.shard_map(
        on_device, mesh=mesh, in_specs=in_specs, out_specs=out_specs, check_vma=False
    )
```

profile of v0, /device:TPU:1, one launch (start us, length us, event | category | flops | bytes accessed | tf_op | source)
XLA Modules:
  0.0 429.6 jit_solution(14055644841048491400)
XLA Ops:
  7.4 1.3 copy-done
  8.6 1.8 fusion.7
  10.6 26.0 %all_to_all.19 = f32[64,3,288]{2,1,0:T(4,128)S(1)} all-to-all(f32[64,3,288]{2,1,0:T(4,128)S(1)} %all_to_all.14), channel_id=1, replica_groups=mesh['kv'=8,'wide'=64] {'wide'}, dimensions={0} | all-to-all | bytes 442368 | tf_op jit(solution)/shard_map/all_to_all | solution.py:79
  36.6 5.1 %copy.53 = f32[3,64,288]{0,2,1:T(8,128)} copy(f32[3,64,288]{2,0,1:T(4,128)S(1)} %bitcast.101) | data formatting | bytes 442368
  41.8 0.5 all-gather.5.cloned.1.call-update
  42.4 0.4 copy-done.1
  42.8 0.2 fusion.2
  43.1 0.3 fusion.5
  43.4 31.5 %all-reduce = (f32[192,24]{0,1:T(8,128)S(1)}, f32[192]{0:T(256)S(1)}) all-reduce(f32[192,24]{0,1:T(8,128)S(1)} %fusion.5, f32[192]{0:T(256)S(1)} %fusion.2), channel_id=1, replica_groups=mesh['kv'=8,'wide'=64] {'kv'}, use_global_device_ids=true, to_apply=%region_3.4 | all-reduce | flops 4800 | bytes 38400 | tf_op jit(solution)/shard_map/psum | solution.py:75
  75.1 43.6 %all_gather.14 = bf16[64,2,8,128]{3,2,1,0:T(8,128)(2,1)S(1)} all-gather(bf16[1,2,8,128]{3,2,1,0:T(8,128)(2,1)S(1)} %copy-done.5), channel_id=1, replica_groups=mesh['kv'=8,'wide'=64] {'wide'}, dimensions={0}, use_global_device_ids=true | all-gather | bytes 266240 | tf_op jit(solution)/shard_map/all_gather | solution.py:85
  118.7 48.5 %all-gather.1 = bf16[64,192,24]{1,2,0:T(8,128)(2,1)S(1)} all-gather(bf16[1,192,24]{1,2,0:T(8,128)(2,1)S(1)} %fusion.25), channel_id=2, replica_groups=mesh['kv'=8,'wide'=64] {'wide'}, dimensions={0}, use_global_device_ids=true | all-gather | bytes 599040 | tf_op jit(solution)/shard_map/all_gather | solution.py:83
  167.2 0.2 constant_dynamic-slice_fusion.1
  168.1 1.6 copy.52
  169.7 4.0 convolution_bitcast_fusion.1
  174.3 0.3 fusion.52
  175.1 49.0 %all-gather.2 = bf16[64,3,2048]{2,1,0:T(4,128)(2,1)S(1)} all-gather(bf16[1,3,2048]{2,1,0:T(4,128)(2,1)S(1)} %reshape.282), channel_id=1, replica_groups=mesh['kv'=8,'wide'=64] {'wide'}, dimensions={0}, use_global_device_ids=true | all-gather | bytes 798720 | tf_op jit(solution)/shard_map/all_gather | solution.py:140
  224.1 0.7 reshape.283
  224.8 0.3 fusion.22
  225.1 10.9 %psum.23 = f32[192,8]{0,1:T(8,128)S(1)} all-reduce(f32[192,8]{0,1:T(8,128)S(1)} %fusion.22), channel_id=1, replica_groups=mesh['kv'=8,'wide'=64] {'kv'}, use_global_device_ids=true, to_apply=%region_8.9 | all-reduce | flops 1536 | bytes 12288 | tf_op jit(solution)/shard_map/psum | solution.py:151
  236.0 2.2 convolution_convert_fusion
  238.4 1.6 convolution_bitcast_fusion
  240.0 29.3 %reduce-scatter.6.cloned.1.call-done = bf16[24,256]{1,0:T(8,128)(2,1)} async-done(((bf16[192,256]{1,0:T(8,128)(2,1)}), bf16[24,256]{1,0:T(8,128)(2,1)}) %reduce-scatter.6.cloned.1.call-update) | async-done | bytes 12304 | tf_op jit(solution)/shard_map/reduce_scatter | solution.py:148
  269.4 151.8 %reduce-scatter.8.cloned.1.call-done = f32[256,24]{0,1:T(8,128)} async-done(((f32[16384,24]{0,1:T(8,128)}), f32[256,24]{0,1:T(8,128)}) %reduce-scatter.8.cloned.1.call-update) | async-done | bytes 24592 | tf_op jit(solution)/shard_map/reduce_scatter | solution.py:157
  421.2 1.3 fusion.24
  (58 shorter events, 2.2 us)
Async XLA Ops:
  7.4 1.3 copy-start
  7.4 160.7 %reduce-scatter.10.cloned.1.call-start = ((), (), s32[]{:S(2)}) async-start(), calls=%async_computation.7 | async-start | bytes 10616832
  41.7 0.7 copy-start.8
  41.7 1.1 copy-start.1
  41.7 1.4 copy-start.10
  41.7 1.4 copy-start.11
  41.7 33.2 %copy-start.6 = (s32[192]{0:T(256)S(1)}, s32[192]{0:T(256)}, u32[]{:S(2)}) copy-start(s32[192]{0:T(256)} %param.25) | copy-start | bytes 2308
  41.7 33.2 %copy-start.7 = (s32[64]{0:T(128)S(1)}, s32[64]{0:T(128)}, u32[]{:S(2)}) copy-start(s32[64]{0:T(128)} %param.26) | copy-start | bytes 772
  41.7 33.4 %copy-start.5 = (bf16[1,2,8,128]{3,2,1,0:T(8,128)(2,1)S(1)}, bf16[1,2,8,128]{3,2,1,0:T(8,128)(2,1)}, u32[]{:S(2)}) copy-start(bf16[1,2,8,128]{3,2,1,0:T(8,128)(2,1)} %param.22) | copy-start | bytes 12292
  41.7 128.0 %all-gather.5.cloned.1.call-start = ((), (), s32[]{:S(2)}) async-start(), calls=%async_computation.4 | async-start | bytes 2129920 | tf_op jit(solution)/shard_map/all_gather | solution.py:84
  42.3 227.0 %reduce-scatter.6.cloned.1.call-start = ((), (), s32[]{:S(2)}) async-start(), calls=%async_computation.5 | async-start | bytes 110592 | tf_op jit(solution)/shard_map/reduce_scatter | solution.py:148
  169.7 4.6 %copy-start.2 = (bf16[3,1,512,128]{3,2,1,0:T(8,128)(2,1)S(1)}, bf16[3,1,512,128]{3,2,1,0:T(8,128)(2,1)}, u32[]{:S(2)}) copy-start(bf16[3,1,512,128]{3,2,1,0:T(8,128)(2,1)} %param.18) | copy-start | bytes 1179652
  169.7 5.1 %copy-start.9 = (bf16[3,1,512,128]{3,2,1,0:T(8,128)(2,1)S(1)}, bf16[3,1,512,128]{3,2,1,0:T(8,128)(2,1)}, u32[]{:S(2)}) copy-start(bf16[3,1,512,128]{3,2,1,0:T(8,128)(2,1)} %param.19) | copy-start | bytes 1179652
  175.1 49.7 %copy-start.4 = (bf16[1,2048,8]{1,2,0:T(8,128)(2,1)S(1)}, bf16[1,2048,8]{1,2,0:T(8,128)(2,1)}, u32[]{:S(2)}) copy-start(bf16[1,2048,8]{1,2,0:T(8,128)(2,1)} %param.23) | copy-start | bytes 98308
  224.8 13.6 %copy-start.3 = (bf16[1,8,16384]{2,1,0:T(8,128)(2,1)S(1)}, bf16[1,8,16384]{2,1,0:T(8,128)(2,1)}, u32[]{:S(2)}) copy-start(bf16[1,8,16384]{2,1,0:T(8,128)(2,1)} %param.24) | copy-start | bytes 786436
  238.3 182.9 %reduce-scatter.8.cloned.1.call-start = ((), (), s32[]{:S(2)}) async-start(), calls=%async_computation.6 | async-start | bytes 1597440 | tf_op jit(solution)/shard_map/reduce_scatter | solution.py:157
Sparse Core Ops, SparseCore 0:
  41.8 108.8 reduce-scatter.9
  238.4 30.8 reduce-scatter.5
  274.7 146.4 reduce-scatter.7
Sparse Core Ops, SparseCore 1:
  45.6 83.2 all-gather.4
where the time goes:
time: 434 us; the launch traced here: 430 us
  blocking collectives  209 us (48%)
  waiting for transfers between devices  182 us (42%)
  between operations  14.8 us (3%)
  matrix products  11.4 us (3%)
  local copies, waits for them, and re-layouts  9.69 us (2%)
    reduce_scatter x1, waiting for transfers between devices, on_device(): lax.psum_scatter(jnp.dot(weight_sheet.T, own_shrink.T, preferred_element_...  152 us
    all_gather x1, blocking collectives, on_device(): slice_portion = lax.all_gather(attention_output, 'wide', axis=0, tiled=True)  49 us
    all_gather x1, blocking collectives, on_device(): shrinks = lax.all_gather(shrink_bf[None], 'wide', axis=0, tiled=True)  48.5 us
    all_gather x1, blocking collectives, on_device(): lax.all_gather(key_value_up_weight, 'wide', axis=0, tiled=True)  43.6 us
    psum x1, blocking collectives, on_device(): total_sq, reduced_hidden = lax.psum((partial_sq, partial_reduced), 'kv')  31.5 us
    reduce_scatter x1, waiting for transfers between devices, on_device(): lax.psum_scatter(mixed[:, :out_cols].astype(jnp.bfloat16), 'kv', scatter_...  29.3 us
    all_to_all x1, blocking collectives, on_device(): lax.all_to_all(base_part, 'wide', split_axis=0, concat_axis=1, tiled=True)  26 us
    psum x1, blocking collectives, on_device(): output_reduced = lax.psum(mixed[:, out_cols:], 'kv')  10.9 us
  transfers between devices with their start and end apart: 4, of which 2 were waited for; matrix products, arithmetic and copies ran while one was open for 1% of the time, Pallas kernels for 0%

commit v1 on v0

v1 whole, which is shorter than its diff:
```python
import math

import jax
import jax.numpy as jnp
import numpy as np
from jax import lax
from jax.experimental import pallas as pl
from jax.experimental.pallas import tpu as pltpu
from jax.sharding import PartitionSpec as P

MODEL_WIDTH = 16384
ROPE_BASE = 500000.0
MESH = pl.DeviceIdType.MESH
NT = (((1,), (1,)), ((), ()))
F32 = jnp.float32
BF16 = jnp.bfloat16


def tile_rank(part):
    for shift in (8, 16, 32, 64):
        part = part + pltpu.roll(part, shift, 1)
    return part


def one_hot_rows(rows, first_lane, slots):
    lane = lax.broadcasted_iota(jnp.int32, (24, 128), 1)
    if first_lane:
        rows = pltpu.roll(rows, 128 - first_lane, 1)
    tiled = tile_rank(jnp.where(lane < 8, rows, 0.0))
    group = lax.shift_right_logical(lane, 3)
    return jnp.concatenate(
        [jnp.where(slots == group + 16 * m, tiled, 0.0) for m in range(4)], axis=1
    ).astype(BF16)


def pack_rows(rows):
    return (
        rows[0:8] + pltpu.roll(rows[8:16], 32, 1) + pltpu.roll(rows[16:24], 64, 1)
    )


def unpack_rows(packed):
    return jnp.concatenate(
        [packed, pltpu.roll(packed, 96, 1), pltpu.roll(packed, 64, 1)], axis=0
    )


def layer(
    hidden, gain, weight_t, out_weight, key_cache, value_cache, down_t, query_up,
    key_value_up, out_down_t, out_up, freq, row_adapter, owner_slot, lengths,
    out,
    hid, gain_v, gained, wt, down3, part, tiny, recv1, recv2, ups, oups, u_all, uo_all,
    y_stage, recv_y, x_stage, recv_x, stage5, recv5, heads, keys, values, freq_v,
    att_f, att_b, recv_a, pack_f, lhs, wo, odown3, po, otiny, recv_o1, recv_o2,
    oy_stage, recv_oy, ox_stage, recv_ox,
    load_sem, s1, r1, s2, r2, su, ru, suo, ruo, szu, rzu, szo, rzo, sy, ry, sx, rx,
    s5, r5, sa, ra, sg, rg, sf, rf, so1, ro1, so2, ro2, soy, roy, sox, rox,
    self_sem,
):
    k = lax.axis_index("kv")
    w = lax.axis_index("wide")
    w_hi = lax.div(w, 8)
    w_lo = lax.rem(w, 8)
    x = lax.div(w, 16)
    c = lax.rem(w, 2)
    y = lax.rem(lax.div(w, 2), 8)
    g = 2 * x + c
    chunk_shift = 32 * lax.rem(w_lo, 4)

    wt[0:96, :] = jnp.zeros((96, 2048), BF16)
    wt[288:384, :] = jnp.zeros((96, 2048), BF16)
    down3[...] = jnp.zeros((128, 2048), BF16)
    odown3[...] = jnp.zeros((128, 2048), BF16)

    def load(src, dst, index):
        copy = pltpu.make_async_copy(src, dst, load_sem.at[index])
        copy.start()
        return copy

    load_hidden = [load(hidden, hid, 0), load(gain, gain_v, 1)]
    load_down = [load(down_t.at[0], down3.at[pl.ds(32 * i, 24)], 2 + i) for i in range(3)]
    load_weight = load(weight_t, wt.at[pl.ds(pl.multiple_of(chunk_shift, 32), 288)], 5)
    load_ups = [
        load(query_up.at[0], ups.at[:, pl.ds(0, 2048)], 6),
        load(key_value_up.at[0, 0], ups.at[:, pl.ds(2048, 128)], 7),
        load(key_value_up.at[0, 1], ups.at[:, pl.ds(2176, 128)], 8),
        load(out_up.at[0, :, pl.ds(pl.multiple_of(2048 * k, 2048), 2048)], oups, 9),
    ]
    load_cache = [load(key_cache.at[:, 0], keys, 10), load(value_cache.at[:, 0], values, 11)]
    load_out = [load(out_weight, wo, 12)] + [
        load(out_down_t.at[0], odown3.at[pl.ds(32 * i, 8)], 13 + i) for i in range(3)
    ]
    load_freq = load(freq, freq_v, 16)

    def z_peer(d):
        return (lax.rem(k + d, 8), w)

    def y_peer(d):
        return (k, 16 * x + 2 * lax.rem(y + d, 8) + c)

    def g_peer(d):
        other = lax.rem(g + d, 8)
        return (k, 16 * lax.div(other, 2) + 2 * y + lax.rem(other, 2))

    def t_peer(i):
        return (w_hi, 8 * k + i)

    def before(pos, d, n=8):
        return lax.rem(pos + n - d, n)

    in_set = w_hi == k

    def t_other(i):
        return jnp.logical_or(jnp.logical_not(in_set), w_lo != i)

    barrier = pltpu.get_barrier_semaphore()
    for d in range(1, 8):
        for peer in (z_peer(d), y_peer(d), g_peer(d)):
            pl.semaphore_signal(barrier, inc=1, device_id=peer, device_id_type=MESH)
    for i in range(8):
        @pl.when(t_other(i))
        def _(i=i):
            pl.semaphore_signal(barrier, inc=1, device_id=t_peer(i), device_id_type=MESH)

    def remote(src, dst, send, recv, peer):
        return pltpu.make_async_remote_copy(
            src_ref=src, dst_ref=dst, send_sem=send, recv_sem=recv,
            device_id=peer, device_id_type=MESH,
        )

    sent = []

    def send_line(src_of, dst, send, recv, peer_of, pos):
        for d in range(1, 8):
            copy = remote(src_of(d), dst.at[pos], send.at[d], recv.at[d], peer_of(d))
            copy.start()
            sent.append(copy)

    def wait_line(dst, send, recv, peer_of, pos):
        for d in range(1, 8):
            slot = dst.at[before(pos, d)]
            remote(slot, slot, send.at[d], recv.at[d], peer_of(d)).wait_recv()

    def t_copies(src_of, dst, send, recv):
        copies = []
        for i in range(8):
            copies.append(remote(src_of(i), dst, send.at[i], recv.at[w_lo], t_peer(i)))
        return copies

    def t_start(src_of, dst, send, recv, own):
        for i, copy in enumerate(t_copies(src_of, dst, send, recv)):
            @pl.when(t_other(i))
            def _(copy=copy):
                copy.start()

            @pl.when(jnp.logical_not(t_other(i)))
            def _(i=i):
                local = pltpu.make_async_copy(src_of(i), dst, own)
                local.start()
                local.wait()

    def t_wait_recv(slot_of, send, recv):
        for j in range(8):
            slot = slot_of(j)

            @pl.when(t_other(j))
            def _(j=j, slot=slot):
                remote(slot, slot, send.at[j], recv.at[j], t_peer(j)).wait_recv()

    def t_wait_send(src_of, dst, send, recv):
        for i, copy in enumerate(t_copies(src_of, dst, send, recv)):
            @pl.when(t_other(i))
            def _(copy=copy):
                copy.wait_send()

    for copy in load_hidden:
        copy.wait()
    wide_h = hid[...].astype(F32)
    gained[...] = (wide_h * gain_v[...]).astype(BF16)
    squares = jnp.sum(wide_h * wide_h, axis=1, keepdims=True)
    for copy in load_down:
        copy.wait()
    reduced = lax.dot_general(gained[...], down3[...], NT, preferred_element_type=F32)
    lane192 = lax.broadcasted_iota(jnp.int32, (192, 128), 1)
    reduced = jnp.where(lax.rem(lane192, 32) == 24, squares, reduced)
    lane8 = lax.broadcasted_iota(jnp.int32, (8, 128), 1)
    for b in range(8):
        r = 24 * b
        tiny[b] = jnp.where(
            lane8 < 32, reduced[r : r + 8],
            jnp.where(lane8 < 64, reduced[r + 8 : r + 16],
                      jnp.where(lane8 < 96, reduced[r + 16 : r + 24], 0.0)),
        )
    recv1[k] = tiny[k]

    pl.semaphore_wait(barrier, jnp.where(in_set, 28, 29))
    send_line(lambda d: tiny.at[lax.rem(k + d, 8)], recv1, s1, r1, z_peer, k)

    for copy in load_ups:
        copy.wait()

    def up_chunk(i):
        return ups.at[:, pl.ds(128 * (2 * i + i // 4), 384)]

    def oup_chunk(i):
        return oups.at[:, pl.ds(256 * i, 256)]

    t_start(up_chunk, u_all.at[w], su, ru, self_sem.at[0])

    load_weight.wait()
    part[...] = lax.dot_general(
        gained[...], wt[...], NT, preferred_element_type=F32
    ).reshape(8, 24, 384)
    send_line(lambda d: part.at[lax.rem(k + d, 8)], recv2, s2, r2, z_peer, k)
    recv2[k] = part[k]

    t_start(oup_chunk, uo_all.at[w], suo, ruo, self_sem.at[1])
    t_wait_recv(lambda j: u_all.at[8 * k + j], su, ru)
    own_u = u_all.at[pl.ds(8 * k, 8)]
    for d in range(1, 8):
        copy = remote(own_u, own_u, szu.at[d], rzu.at[d], z_peer(d))
        copy.start()
        sent.append(copy)

    row24 = lax.broadcasted_iota(jnp.int32, (24, 128), 0)
    slots = jnp.zeros((24, 128), jnp.int32)
    slots_o = jnp.zeros((24, 128), jnp.int32)
    for b in range(24):
        slot = owner_slot[row_adapter[24 * k + b]]
        yy, cc, rr = b // 6, (b // 3) % 2, b % 3
        slots = jnp.where(row24 == b, slot, slots)
        slots_o = jnp.where(row24 == 12 * cc + 3 * yy + rr, slot, slots_o)
    lane24 = lax.broadcasted_iota(jnp.int32, (24, 128), 1)

    wait_line(recv1, s1, r1, z_peer, k)
    rows = unpack_rows(jnp.sum(recv1[...], axis=0))
    scale = lax.rsqrt(rows[:, 24:25] / MODEL_WIDTH + 1e-05)
    rows = (rows * scale).astype(BF16).astype(F32)
    rows = jnp.where(jnp.logical_and(slots == w, lane24 < 24), rows, 0.0)
    y_stage[...] = pack_rows(rows)
    send_line(lambda d: y_stage, recv_y, sy, ry, y_peer, y)
    recv_y[y] = y_stage[...]
    wait_line(recv_y, sy, ry, y_peer, y)
    x_stage[...] = jnp.sum(recv_y[...], axis=0)
    send_line(lambda d: x_stage, recv_x, sx, rx, g_peer, g)
    recv_x[g] = x_stage[...]
    wait_line(recv_x, sx, rx, g_peer, g)
    shrink = unpack_rows(jnp.sum(recv_x[...], axis=0))
    left_q = one_hot_rows(shrink, 0, slots)
    left_k = one_hot_rows(shrink, 8, slots)
    left_v = one_hot_rows(shrink, 16, slots)

    for d in range(1, 8):
        slot = u_all.at[pl.ds(8 * before(k, d), 8)]
        remote(slot, slot, szu.at[d], rzu.at[d], z_peer(d)).wait_recv()
    u_mat = u_all[...].reshape(512, 384)
    delta = jnp.dot(left_q, u_mat, preferred_element_type=F32)
    delta_k = jnp.dot(left_k, u_mat[:, 128:256], preferred_element_type=F32)
    delta_v = jnp.dot(left_v, u_mat[:, 256:384], preferred_element_type=F32)
    last = w_lo == 7
    delta = jnp.concatenate(
        [
            delta[:, 0:128],
            jnp.where(last, delta_k, delta[:, 128:256]),
            jnp.where(last, delta_v, delta[:, 256:384]),
        ],
        axis=1,
    )
    lane384 = lax.broadcasted_iota(jnp.int32, (24, 384), 1)
    inside = jnp.logical_and(lane384 >= chunk_shift, lane384 < chunk_shift + 288)
    wait_line(recv2, s2, r2, z_peer, k)
    base = jnp.sum(recv2[...], axis=0) * scale
    merged = base + 2.0 * jnp.where(inside, delta, 0.0)
    for i in range(8):
        for t in range(3):
            stage5[i, :, t, :] = merged[3 * i : 3 * i + 3, 128 * t : 128 * t + 128]
    t_start(lambda i: stage5.at[i], recv5.at[w_lo], s5, r5, self_sem.at[2])

    t_wait_recv(lambda j: uo_all.at[8 * k + j], suo, ruo)
    own_uo = uo_all.at[pl.ds(8 * k, 8)]
    for d in range(1, 8):
        copy = remote(own_uo, own_uo, szo.at[d], rzo.at[d], z_peer(d))
        copy.start()
        sent.append(copy)

    load_freq.wait()
    for copy in load_cache:
        copy.wait()
    lane1 = lax.broadcasted_iota(jnp.int32, (1, 128), 1)
    turns = []
    for r in range(3):
        angle = lengths[r].astype(F32) * freq_v[...]
        sine = jnp.sin(angle)
        turns.append((jnp.cos(angle), jnp.where(lane1 < 64, -sine, sine)))
    t_wait_recv(lambda j: recv5.at[j], s5, r5)
    heads[...] = jnp.zeros((3, 24, 128), F32)
    for j in range(8):
        t = 2 * j + j // 4
        heads[:, t : t + 3, :] += recv5[j]
    root = 1.0 / math.sqrt(128.0)
    slot512 = lax.broadcasted_iota(jnp.int32, (16, 512), 1)
    for r in range(3):
        cosine, sine = turns[r]
        raw = heads[r]
        turned = (raw * cosine + pltpu.roll(raw, 64, 1) * sine).astype(BF16)
        query = turned[0:16]
        key_new = turned[16:17].astype(F32)
        value_new = raw[17:18].astype(BF16).astype(F32)
        scores = lax.dot_general(query, keys[r], NT, preferred_element_type=F32) * root
        scores = jnp.where(slot512 < lengths[r], scores, -jnp.inf)
        fresh = jnp.sum(query.astype(F32) * key_new, axis=1, keepdims=True) * root
        top = jnp.maximum(jnp.max(scores, axis=1, keepdims=True), fresh)
        expd = jnp.exp(scores - top)
        exp_new = jnp.exp(fresh - top)
        total = jnp.sum(expd, axis=1, keepdims=True) + exp_new
        probs = (expd / total).astype(BF16)
        prob_new = (exp_new / total).astype(BF16).astype(F32)
        attended = jnp.dot(probs, values[r], preferred_element_type=F32)
        attended = attended + prob_new * value_new
        for h in range(16):
            att_f[r : r + 1, 128 * h : 128 * h + 128] = attended[h : h + 1]
    att_f[3:4, :] = jnp.zeros((1, 2048), F32)
    att_b[...] = att_f[...].astype(BF16)

    send_line(lambda d: att_b, recv_a, sa, ra, y_peer, y)
    recv_a[y] = att_b[...]
    wait_line(recv_a, sa, ra, y_peer, y)
    for j in range(8):
        pack_f[3 * j : 3 * j + 3, :] = recv_a[j].astype(F32)[0:3]
    lhs[g] = pack_f[...].astype(BF16)
    sibling = (k, 16 * x + 2 * y + 1 - c)
    own = lhs.at[g]
    forward = []
    for d in range(1, 4):
        peer = (k, 16 * lax.rem(x + d, 4) + 2 * y + c)
        forward.append(remote(own, own, sg.at[d], rg.at[d], peer))
    forward.append(remote(own, own, sg.at[0], rg.at[0], sibling))
    for copy in forward:
        copy.start()
        sent.append(copy)
    for d in range(1, 4):
        far = before(x, d, 4)
        slot = lhs.at[2 * far + c]
        remote(slot, slot, sg.at[d], rg.at[d], sibling).wait_recv()
        copy = remote(slot, slot, sf.at[d], rf.at[d], sibling)
        copy.start()
        sent.append(copy)
    slot = lhs.at[2 * x + 1 - c]
    remote(slot, slot, sg.at[0], rg.at[0], sibling).wait_recv()
    for d in range(1, 4):
        slot = lhs.at[2 * before(x, d, 4) + 1 - c]
        remote(slot, slot, sf.at[d], rf.at[d], sibling).wait_recv()

    for copy in load_out:
        copy.wait()
    all_rows = lhs[...].reshape(192, 2048)
    oreduced = lax.dot_general(all_rows, odown3[...], NT, preferred_element_type=F32)

    def block_rows(array, b):
        r = 48 * (b // 2) + 12 * (b % 2)
        return jnp.concatenate([array[r : r + 12], array[r + 24 : r + 36]], axis=0)

    for b in range(8):
        mine = block_rows(oreduced, b)
        otiny[b] = jnp.where(
            lane8 < 32, mine[0:8],
            jnp.where(lane8 < 64, mine[8:16], jnp.where(lane8 < 96, mine[16:24], 0.0)),
        )
    send_line(lambda d: otiny.at[lax.rem(k + d, 8)], recv_o1, so1, ro1, z_peer, k)
    recv_o1[k] = otiny[k]
    product = jnp.dot(all_rows, wo[...], preferred_element_type=F32)
    for b in range(8):
        po[b] = block_rows(product, b).astype(BF16)
    send_line(lambda d: po.at[lax.rem(k + d, 8)], recv_o2, so2, ro2, z_peer, k)
    recv_o2[k] = po[k]

    wait_line(recv_o1, so1, ro1, z_peer, k)
    rows = unpack_rows(jnp.sum(recv_o1[...], axis=0)).astype(BF16).astype(F32)
    rows = jnp.where(jnp.logical_and(slots_o == w, lane24 < 8), rows, 0.0)
    oy_stage[...] = pack_rows(rows)
    send_line(lambda d: oy_stage, recv_oy, soy, roy, y_peer, y)
    recv_oy[y] = oy_stage[...]
    wait_line(recv_oy, soy, roy, y_peer, y)
    ox_stage[...] = jnp.sum(recv_oy[...], axis=0)
    send_line(lambda d: ox_stage, recv_ox, sox, rox, g_peer, g)
    recv_ox[g] = ox_stage[...]
    wait_line(recv_ox, sox, rox, g_peer, g)
    oshrink = unpack_rows(jnp.sum(recv_ox[...], axis=0))
    left_o = one_hot_rows(oshrink, 0, slots_o)
    for d in range(1, 8):
        slot = uo_all.at[pl.ds(8 * before(k, d), 8)]
        remote(slot, slot, szo.at[d], rzo.at[d], z_peer(d)).wait_recv()
    change = jnp.dot(left_o, uo_all[...].reshape(512, 256), preferred_element_type=F32)
    wait_line(recv_o2, so2, ro2, z_peer, k)
    total_out = jnp.sum(recv_o2[...].astype(F32), axis=0) + 2.0 * change
    to = lax.broadcasted_iota(jnp.int32, (24, 24), 0)
    frm = lax.broadcasted_iota(jnp.int32, (24, 24), 1)
    want = 12 * lax.rem(lax.div(to, 3), 2) + 3 * lax.div(to, 6) + lax.rem(to, 3)
    order = jnp.where(frm == want, 1.0, 0.0).astype(BF16)
    out[...] = jnp.dot(order, total_out.astype(BF16), preferred_element_type=F32).astype(BF16)

    for copy in sent:
        copy.wait_send()
    t_wait_send(up_chunk, u_all.at[w], su, ru)
    t_wait_send(oup_chunk, uo_all.at[w], suo, ruo)
    t_wait_send(lambda i: stage5.at[i], recv5.at[w_lo], s5, r5)


SCRATCH = [
    ((192, 2048), BF16), ((1, 2048), F32), ((192, 2048), BF16), ((384, 2048), BF16),
    ((128, 2048), BF16), ((8, 24, 384), F32), ((8, 8, 128), F32), ((8, 8, 128), F32),
    ((8, 24, 384), F32), ((8, 2304), BF16), ((8, 2048), BF16), ((64, 8, 384), BF16),
    ((64, 8, 256), BF16),
    ((8, 128), F32), ((8, 8, 128), F32), ((8, 128), F32), ((8, 8, 128), F32),
    ((8, 3, 3, 128), F32), ((8, 3, 3, 128), F32), ((3, 24, 128), F32),
    ((3, 512, 128), BF16), ((3, 512, 128), BF16), ((1, 128), F32),
    ((4, 2048), F32), ((4, 2048), BF16), ((8, 4, 2048), BF16), ((24, 2048), F32),
    ((8, 24, 2048), BF16), ((2048, 256), BF16), ((128, 2048), BF16),
    ((8, 24, 256), BF16), ((8, 8, 128), F32), ((8, 8, 128), F32), ((8, 24, 256), BF16),
    ((8, 128), F32), ((8, 8, 128), F32), ((8, 128), F32), ((8, 8, 128), F32),
]


def on_device(
    hidden_input, input_norm_gain, joint_projection_weight, output_weight, key_cache,
    value_cache, joint_down_weight, query_up_weight, key_value_up_weight,
    output_down_weight, output_up_weight, row_adapter_index, adapter_owner_slot, lengths,
):
    half = np.arange(64, dtype=np.float64)
    freq = np.float64(ROPE_BASE) ** (-half * 2.0 / 128.0)
    freq = jnp.asarray(np.concatenate([freq, freq])[None, :].astype(np.float32))
    any_spec = pl.BlockSpec(memory_space=pl.ANY)
    smem_spec = pl.BlockSpec(memory_space=pltpu.SMEM)
    sems = [pltpu.SemaphoreType.DMA((17,))] + [pltpu.SemaphoreType.DMA((8,))] * 33
    return pl.pallas_call(
        layer,
        out_shape=jax.ShapeDtypeStruct((24, 256), BF16),
        in_specs=[any_spec] * 12 + [smem_spec] * 3,
        out_specs=pl.BlockSpec(memory_space=pltpu.VMEM),
        scratch_shapes=[pltpu.VMEM(s, t) for s, t in SCRATCH] + sems,
        compiler_params=pltpu.CompilerParams(
            collective_id=0, has_side_effects=True, vmem_limit_bytes=40 * 1024 * 1024
        ),
        cost_estimate=pl.CostEstimate(
            flops=500_000_000, bytes_accessed=5_000_000, transcendentals=30_000
        ),
        name="layer",
    )(
        hidden_input, input_norm_gain[None, :], joint_projection_weight.T, output_weight,
        key_cache, value_cache, jnp.swapaxes(joint_down_weight, 1, 2), query_up_weight,
        key_value_up_weight, jnp.swapaxes(output_down_weight, 1, 2), output_up_weight,
        freq, row_adapter_index, adapter_owner_slot, lengths,
    )


def solution(mesh):
    in_specs = (
        P(None, "kv"), P("kv"), P("kv", "wide"), P("kv", "wide"),
        P("wide", "kv", None, None), P("wide", "kv", None, None), P("wide", "kv", None),
        P("wide", None, "kv"), P("wide", None, None, "kv"), P("wide", "kv", None),
        P("wide", None, None), P(), P(), P("wide"),
    )
    return jax.shard_map(
        on_device, mesh=mesh, in_specs=in_specs, out_specs=P("kv", "wide"), check_vma=False
    )
```

time: 434 us -> 97.1 us (0.22)
  blocking collectives: 209 us -> 0 us
  waiting for transfers between devices: 182 us -> 0 us
  Pallas kernels: 0 us -> 82.9 us
  between operations: 14.8 us -> 0.02 us
  matrix products: 11.4 us -> 0 us
    reduce_scatter x2 -> x0, waiting for transfers between devices: 181 us -> none  [the longest x1 152 us: on_device(): lax.psum_scatter(jnp.dot(weight_sheet.T, own_shrink.T, preferred_element_...]
    all_gather x3 -> x0, blocking collectives: 141 us -> none  [the longest x1 49 us: on_device(): slice_portion = lax.all_gather(attention_output, 'wide', axis=0, tiled=True)]
    pallas_call x0 -> x1, Pallas kernels: none -> 82.9 us  [on_device(): pl.pallas_call(layer, out_shape=jax.ShapeDtypeStruct((24, 256), BF16), in...]
    psum x2 -> x0, blocking collectives: 42.4 us -> none  [the longest x1 31.5 us: on_device(): total_sq, reduced_hidden = lax.psum((partial_sq, partial_reduced), 'kv')]
    all_to_all x1 -> x0, blocking collectives: 26 us -> none  [on_device(): lax.all_to_all(base_part, 'wide', split_axis=0, concat_axis=1, tiled=True)]
    dot_general x11 -> x0, matrix products: 11.4 us -> none  [the longest x1 3.96 us: on_device(): jnp.einsum('nbr,nrc->bc', own_rows[:, :, :rank_width], query_sheet, prefe...]
    unnamed x30 -> x31, local copies, waits for them, and re-layouts: 9.14 us -> 13.6 us
  transfers between devices with their start and end apart: 4 -> 0, of which waited for: 2 -> 0; matrix products, arithmetic and copies ran while one was open for 1% -> 0% of each run, Pallas kernels for 0% -> 0%
where the time goes in v1:
time: 97.1 us; the launch traced here: 96.5 us
  Pallas kernels  82.9 us (85%)
  local copies, waits for them, and re-layouts  13.6 us (14%)
    pallas_call x1, Pallas kernels, on_device(): pl.pallas_call(layer, out_shape=jax.ShapeDtypeStruct((24, 256), BF16), in...  82.9 us
    unnamed x31, local copies, waits for them, and re-layouts  13.6 us

profile of v1, /device:TPU:1, one launch (start us, length us, event | category | flops | bytes accessed | tf_op | source)
XLA Modules:
  0.0 96.5 jit_solution(1320688768066840463)
XLA Ops:
  0.0 0.0 copy-start
  0.0 1.3 %copy-done = bf16[2048,288]{0,1:T(8,128)(2,1)S(1)} copy-done((bf16[2048,288]{0,1:T(8,128)(2,1)S(1)}, bf16[2048,288]{0,1:T(8,128)(2,1)}, u32[]{:S(2)}) %copy-start) | copy-done | bytes 1179672
  1.3 0.0 copy-start.1
  1.3 1.2 %copy-done.1 = bf16[2048,256]{1,0:T(8,128)(2,1)S(1)} copy-done((bf16[2048,256]{1,0:T(8,128)(2,1)S(1)}, bf16[2048,256]{1,0:T(8,128)(2,1)}, u32[]{:S(2)}) %copy-start.1) | copy-done | bytes 1048600
  2.5 0.0 copy-start.2
  2.5 1.1 %copy-done.2 = bf16[192,2048]{1,0:T(8,128)(2,1)S(1)} copy-done((bf16[192,2048]{1,0:T(8,128)(2,1)S(1)}, bf16[192,2048]{1,0:T(8,128)(2,1)}, u32[]{:S(2)}) %copy-start.2) | copy-done | bytes 786456
  3.6 0.0 copy-start.3
  3.6 1.0 %copy-done.3 = bf16[3,1,512,128]{3,2,1,0:T(8,128)(2,1)S(1)} copy-done((bf16[3,1,512,128]{3,2,1,0:T(8,128)(2,1)S(1)}, bf16[3,1,512,128]{3,2,1,0:T(8,128)(2,1)}, u32[]{:S(2)}) %copy-start.3) | copy-done | bytes 393240
  4.6 0.0 copy-start.4
  4.6 1.0 %copy-done.4 = bf16[3,1,512,128]{3,2,1,0:T(8,128)(2,1)S(1)} copy-done((bf16[3,1,512,128]{3,2,1,0:T(8,128)(2,1)S(1)}, bf16[3,1,512,128]{3,2,1,0:T(8,128)(2,1)}, u32[]{:S(2)}) %copy-start.4) | copy-done | bytes 393240
  5.6 0.0 copy-start.5
  5.6 0.9 copy-done.5
  6.6 0.0 copy-start.6
  6.6 0.9 copy-done.6
  7.5 0.8 copy-done.7
  8.2 0.8 copy-done.8
  9.0 0.7 copy-done.9
  9.7 0.7 copy-done.10
  10.4 0.7 copy-done.11
  11.1 0.7 copy-done.12
  11.7 0.7 copy-done.13
  12.4 0.7 copy-done.14
  13.0 82.9 %layer.1 = bf16[24,256]{1,0:T(8,128)(2,1)S(1)} custom-call(bf16[192,2048]{1,0:T(8,128)(2,1)S(1)} %copy-done.2, f32[1,2048]{1,0:T(1,128)S(1)} %bitcast.7, bf16[288,2048]{1,0:T(8,128)(2,1)S(1)} %bitcast.4, bf16[2048,256]{1,0:T(8,128)(2,1)S(1)} %copy-done.1, bf16[3,1,512,128]{3,2,1,0:T(8,128)(2,1)S(1)} %copy-done.3, bf16[3,1,512,128]{3,2,1,0:T(8,128)(2,1)S(1)} %copy-done.4, ...), custom_call_target="tpu_custom_call" | custom-call | flops 500000000 | bytes 5000000 | tf_op jit(solution)/shard_map/layer/pallas_call | solution.py:435
  95.9 0.6 copy.17
  (8 shorter events, 0.0 us)
Async XLA Ops:
  0.0 1.3 %copy-start = (bf16[2048,288]{0,1:T(8,128)(2,1)S(1)}, bf16[2048,288]{0,1:T(8,128)(2,1)}, u32[]{:S(2)}) copy-start(bf16[2048,288]{0,1:T(8,128)(2,1)} %param.17) | copy-start | bytes 3538948
  1.3 1.2 %copy-start.1 = (bf16[2048,256]{1,0:T(8,128)(2,1)S(1)}, bf16[2048,256]{1,0:T(8,128)(2,1)}, u32[]{:S(2)}) copy-start(bf16[2048,256]{1,0:T(8,128)(2,1)} %out_weight.1) | copy-start | bytes 3145732
  2.5 1.1 %copy-start.2 = (bf16[192,2048]{1,0:T(8,128)(2,1)S(1)}, bf16[192,2048]{1,0:T(8,128)(2,1)}, u32[]{:S(2)}) copy-start(bf16[192,2048]{1,0:T(8,128)(2,1)} %hidden.1) | copy-start | bytes 2359300
  3.6 1.0 %copy-start.3 = (bf16[3,1,512,128]{3,2,1,0:T(8,128)(2,1)S(1)}, bf16[3,1,512,128]{3,2,1,0:T(8,128)(2,1)}, u32[]{:S(2)}) copy-start(bf16[3,1,512,128]{3,2,1,0:T(8,128)(2,1)} %key_cache.1) | copy-start | bytes 1179652
  4.6 1.0 %copy-start.4 = (bf16[3,1,512,128]{3,2,1,0:T(8,128)(2,1)S(1)}, bf16[3,1,512,128]{3,2,1,0:T(8,128)(2,1)}, u32[]{:S(2)}) copy-start(bf16[3,1,512,128]{3,2,1,0:T(8,128)(2,1)} %value_cache.1) | copy-start | bytes 1179652
  5.6 0.9 copy-start.5
  6.6 0.9 copy-start.6
  7.5 0.8 copy-start.7
  8.2 0.8 copy-start.8
  9.0 0.7 copy-start.9
  9.7 0.7 copy-start.10
  10.4 0.7 copy-start.11
  11.0 0.7 copy-start.12
  11.7 0.7 copy-start.13
  12.4 0.7 copy-start.14
